TPU v7x, 256 devices: a whole 4x4x8 slice. The times are simulated.
256 devices in a mesh: seq: 128 (over z, x, y), head: 2 (over core).
Axes of the slice: x: 4, y: 4, z: 8, core: 2. Of those that a mesh axis runs over, the one named last changes fastest.
Arguments:
- queries: bfloat16 [32768, 4096], P('seq', 'head'), may hold values from -300 to 300
- keys: bfloat16 [32768, 512], P('seq', 'head'), may hold values from -8 to 8
- values: bfloat16 [32768, 512], P('seq', 'head'), may hold values from -24 to 24
- kept_count: int32 [128, 4], P('seq', 'head'), may hold values from 0 to 128, as said below
- kept_rows: int32 [128, 4, 128], P('seq', 'head'), may hold values from 0 to 255, as said below
Outputs:
- attended: bfloat16 [32768, 4096], P('seq', 'head')
Inputs may be any that keep to these rules, and one draw needn't show every extreme that they name: `kept_count`: for each block and each index of head, exactly one of its 2 KV heads has 128 retained rows and the others have none. `kept_rows`: for each block and KV head, distinct rows in increasing order.
All inputs are finite; a program needn't handle non-finite values.
Results may differ from a plain program's by a relative error of at most 0.0055.
Values may be sent and summed in bfloat16 or wider, within the bound.
A program may use at most 64 MiB of HBM per device.

v0:
```python
import math

import jax
import jax.numpy as jnp
from jax import lax
from jax.sharding import PartitionSpec as P

HD = 128
ANCHOR = 128


masked_score = -1e30


def from_root(value, axis, source):
    kept = jnp.where(lax.axis_index(axis) == source, value, 0).astype(value.dtype)
    return lax.psum(kept, axis)


def absorb(running, block_scores, value_rows, form):
    run_max, run_total, run_accum = running
    new_max = jnp.maximum(run_max, jnp.max(block_scores, axis=-1))
    shrink = jnp.exp(run_max - new_max)
    weights = jnp.exp(block_scores - new_max[..., None])
    run_total = run_total * shrink + jnp.sum(weights, axis=-1)
    run_accum = run_accum * shrink[..., None] + jnp.einsum(
        form, weights.astype(jnp.bfloat16), value_rows, preferred_element_type=jnp.float32
    )
    return (new_max, run_total, run_accum)


def per_device(queries, keys, values, kept_count, kept_rows):
    tok_rows = queries.shape[0]
    kv_local = keys.shape[1] // HD
    group_size = queries.shape[1] // keys.shape[1]
    host_count = lax.axis_size("seq")
    my_host = lax.axis_index("seq")
    score_scale = 1.0 / math.sqrt(HD)
    query_heads = jnp.transpose(queries.reshape(tok_rows, kv_local, group_size, HD), (1, 2, 0, 3))
    key_heads = keys.reshape(tok_rows, kv_local, HD)
    value_heads = values.reshape(tok_rows, kv_local, HD)
    anchor_pair = from_root(jnp.stack([keys[:ANCHOR], values[:ANCHOR]]), "seq", 0)
    local_scores = (
        jnp.einsum("gjtd,sgd->gjts", query_heads, key_heads, preferred_element_type=jnp.float32)
        * score_scale
    )
    causal = lax.broadcasted_iota(jnp.int32, (tok_rows, tok_rows), 0) >= lax.broadcasted_iota(
        jnp.int32, (tok_rows, tok_rows), 1
    )
    local_scores = jnp.where(causal, local_scores, masked_score)
    run_max = jnp.max(local_scores, axis=-1)
    local_weights = jnp.exp(local_scores - run_max[..., None])
    run_total = jnp.sum(local_weights, axis=-1)
    run_accum = jnp.einsum(
        "gjts,sgd->gjtd",
        local_weights.astype(jnp.bfloat16),
        value_heads,
        preferred_element_type=jnp.float32,
    )
    running = (run_max, run_total, run_accum)
    anchor_keys = anchor_pair[0].reshape(ANCHOR, kv_local, HD)
    anchor_values = anchor_pair[1].reshape(ANCHOR, kv_local, HD)
    anchor_scores = (
        jnp.einsum("gjtd,sgd->gjts", query_heads, anchor_keys, preferred_element_type=jnp.float32)
        * score_scale
    )
    anchor_scores = jnp.where(my_host >= 1, anchor_scores, masked_score)
    running = absorb(running, anchor_scores, anchor_values, "gjts,sgd->gjtd")
    local_ids = jnp.arange(kv_local, dtype=jnp.int32)
    owner_head = jnp.sum(jnp.where(kept_count[0] > 0, local_ids, 0))
    chosen_rows = lax.dynamic_index_in_dim(kept_rows[0], owner_head, 0, keepdims=False)
    own_keys = lax.dynamic_index_in_dim(key_heads[chosen_rows], owner_head, 1, keepdims=False)
    own_values = lax.dynamic_index_in_dim(value_heads[chosen_rows], owner_head, 1, keepdims=False)
    own_block = jnp.stack([own_keys, own_values])[None]
    owner_tag = owner_head.reshape(1)
    every_block, every_tag = (
        lax.all_gather(own_block, "seq", axis=0, tiled=True),
        lax.all_gather(owner_tag, "seq", axis=0, tiled=True),
    )
    host_ids = jnp.arange(host_count, dtype=jnp.int32)
    earlier = host_ids < my_host
    hosts_per_turn = 8
    run_max, run_total, run_accum = running
    for head_pos in range(kv_local):
        is_mine = earlier & (every_tag == head_pos)
        live_count = jnp.sum(is_mine.astype(jnp.int32))
        order = jnp.argsort(jnp.where(is_mine, host_ids, host_ids + host_count))
        group_queries = query_heads[head_pos]

        def visit(
            turn, head_state, group_queries=group_queries, order=order, live_count=live_count
        ):
            picks = lax.dynamic_slice_in_dim(order, turn * hosts_per_turn, hosts_per_turn)
            slot_live = (
                turn * hosts_per_turn + jnp.arange(hosts_per_turn, dtype=jnp.int32) < live_count
            )
            chosen = every_block[picks]
            batch_keys = chosen[:, 0].reshape(-1, HD)
            batch_values = chosen[:, 1].reshape(-1, HD)
            block_scores = (
                jnp.einsum(
                    "jtd,sd->jts", group_queries, batch_keys, preferred_element_type=jnp.float32
                )
                * score_scale
            )
            key_live = jnp.repeat(slot_live, chosen.shape[2])
            block_scores = jnp.where(key_live, block_scores, masked_score)
            return absorb(head_state, block_scores, batch_values, "jts,sd->jtd")

        turns = (live_count + hosts_per_turn - 1) // hosts_per_turn
        head_state = (run_max[head_pos], run_total[head_pos], run_accum[head_pos])
        head_state = lax.fori_loop(0, turns, visit, head_state)
        run_max = run_max.at[head_pos].set(head_state[0])
        run_total = run_total.at[head_pos].set(head_state[1])
        run_accum = run_accum.at[head_pos].set(head_state[2])
    running = (run_max, run_total, run_accum)
    run_max, run_total, run_accum = running
    mixed = run_accum / run_total[..., None]
    return (
        jnp.transpose(mixed, (2, 0, 1, 3))
        .reshape(tok_rows, kv_local * group_size * HD)
        .astype(jnp.bfloat16)
    )


def solution(mesh):
    return jax.shard_map(
        per_device,
        mesh=mesh,
        in_specs=(
            P("seq", "head"),
            P("seq", "head"),
            P("seq", "head"),
            P("seq", "head"),
            P("seq", "head", None),
        ),
        out_specs=P("seq", "head"),
        check_vma=False,
    )
```

profile of v0, /device:TPU:228, one launch (start us, length us, event | category | flops | bytes accessed | tf_op | source)
XLA Modules:
  0.0 557.7 jit_solution(1240972165963433711)
XLA Ops:
  19.7 21.3 %all-reduce = s32[128]{0:T(128)S(1)} all-reduce(s32[128]{0:T(128)S(1)} %dynamic-update-slice.17), channel_id=1, replica_groups=mesh['seq'=128,'head'=2] {'seq'}, use_global_device_ids=true, to_apply=%add | all-reduce | flops 128 | bytes 1024
  54.4 168.8 %all-reduce.3.cloned.1.call-done = bf16[2,128,256]{1,2,0:T(8,128)(2,1)} async-done(((bf16[2,128,256]{1,2,0:T(8,128)(2,1)}), bf16[2,128,256]{1,2,0:T(8,128)(2,1)}) %all-reduce.3.cloned.1.call-update) | async-done | bytes 131088 | tf_op jit(solution)/shard_map/psum | solution.py:17
  230.1 118.5 %all-gather.3.cloned.1.call-done = bf16[256,128,128]{2,1,0:T(8,128)(2,1)} async-done(((bf16[2,128,128]{2,1,0:T(8,128)(2,1)}), bf16[256,128,128]{2,1,0:T(8,128)(2,1)}) %all-gather.3.cloned.1.call-update) | async-done | bytes 8388624 | tf_op jit(solution)/shard_map/all_gather | solution.py:77
  348.6 77.6 %while.33 = (s32[]{:T(128)}, f32[8,256]{1,0:T(8,128)S(1)}, f32[8,256]{1,0:T(8,128)S(1)}, f32[8,256,128]{2,1,0:T(8,128)S(1)}, s32[]{:T(128)}, /*index=5*/s32[]{:T...) while((s32[]{:T(128)}, f32[8,256]{1,0:T(8,128)S(1)}, ...), condition=%wide.region_11.12_spmd, body=%wide.region_8.11_spmd.sunk | while | flops 1097339904 | bytes 30548296 | solution.py:112
  348.7 4.0 gather_fusion
  359.8 4.0 gather_fusion
  370.9 4.0 gather_fusion
  382.0 4.0 gather_fusion
  393.0 4.0 gather_fusion
  404.1 4.0 gather_fusion
  415.2 4.0 gather_fusion
  430.4 117.2 %while.34 = (s32[]{:T(128)}, f32[8,256]{1,0:T(8,128)S(1)}, f32[8,256]{1,0:T(8,128)S(1)}, f32[8,256,128]{2,1,0:T(8,128)}, s32[]{:T(128)}, /*index=5*/s32[]{:T(128...) while((s32[]{:T(128)}, f32[8,256]{1,0:T(8,128)S(1)}, ...), condition=%wide.region_17.18_spmd, body=%wide.region_14.17_spmd.sunk | while | flops 1097339904 | bytes 30548296 | solution.py:112
  430.4 4.2 gather_fusion.1
  438.9 4.6 fusion.90
  443.6 4.0 gather_fusion.1
  451.9 4.6 fusion.90
  456.6 4.0 gather_fusion.1
  465.0 4.6 fusion.90
  478.0 4.6 fusion.90
  491.0 4.6 fusion.90
  504.0 4.6 fusion.90
  517.0 4.6 fusion.90
  530.0 4.6 fusion.90
  543.0 4.6 fusion.90
  (235 shorter events, 149.9 us)
Async XLA Ops:
  6.5 216.7 %all-reduce.3.cloned.1.call-start = ((), (), s32[]{:S(2)}) async-start(), calls=%async_computation | async-start | bytes 262144 | tf_op jit(solution)/shard_map/psum | solution.py:17
  9.2 339.5 %all-gather.3.cloned.1.call-start = ((), (), s32[]{:S(2)}) async-start(), calls=%async_computation.1 | async-start | bytes 8454144 | tf_op jit(solution)/shard_map/all_gather | solution.py:77
  223.2 2.1 copy-start.2
  226.1 1.4 copy-start
  430.4 118.8 %copy-start.1 = (f32[2,8,256,128]{2,3,1,0:T(8,128)S(1)}, f32[2,8,256,128]{2,3,1,0:T(8,128)}, u32[]{:S(2)}) copy-start(f32[2,8,256,128]{2,3,1,0:T(8,128)} %bitcast_dynamic-update-slice_fusion.1) | copy-start | bytes 6291460
Sparse Core Ops, SparseCore 0:
  12.8 210.3 all-reduce.2
  227.3 121.3 all-gather.2
where the time goes:
time: 569 us; the launch traced here: 558 us
  waiting for transfers between devices  287 us (50%)
  local copies, waits for them, and re-layouts  88.7 us (16%)
  matrix products  84.9 us (15%)
  other arithmetic  57.7 us (10%)
  blocking collectives  21.3 us (4%)
  between operations  16.6 us (3%)
    psum x1, waiting for transfers between devices, from_root(): return lax.psum(kept, axis)  169 us
    all_gather x1, waiting for transfers between devices, per_device(): lax.all_gather(own_block, 'seq', axis=0, tiled=True)  119 us
    gather x16, local copies, waits for them, and re-layouts, visit(): chosen = every_block[picks]  64.6 us
    dot_general x17, matrix products, absorb(): jnp.einsum(form, weights.astype(jnp.bfloat16), value_rows, preferred_elem...  59.5 us
    reduce_sum x17, other arithmetic, absorb(): run_total = run_total * shrink + jnp.sum(weights, axis=-1)  36.6 us
    dot_general x16, matrix products, visit(): jnp.einsum('jtd,sd->jts', group_queries, batch_keys, preferred_element_ty...  21.5 us
    unnamed x1, blocking collectives  21.3 us
  transfers between devices with their start and end apart: 2, of which 2 were waited for; matrix products, arithmetic and copies ran while one was open for 5% of the time, Pallas kernels for 0%

commit v1 on v0

v1 whole, which is shorter than its diff:
```python
import functools
import math

import jax
import jax.numpy as jnp
from jax import lax
from jax.experimental import pallas as pl
from jax.experimental.pallas import tpu as pltpu
from jax.sharding import PartitionSpec as P

F32 = jnp.float32
BF16 = jnp.bfloat16
HD = 128
TOK = 256
NZ, NX, NY = 8, 4, 4
PLANE = NX * NY
BLK = 272
CB = 8
NK = CB * 128
R = 1024
NR = 2
LOW = -1.0e30
HIGH = 1.0e30
CSC = math.log2(math.e) / math.sqrt(HD)


def dot(a, b):
    return jnp.dot(a, b, preferred_element_type=F32)


def dot_tn(a, b):
    return lax.dot_general(a, b, (((0,), (0,)), ((), ())), preferred_element_type=F32)


def widen(row):
    return jnp.concatenate([row] * (R // 128), axis=1)


def kernel(
    q_ref, k_ref, v_ref, cnt_ref, rows_ref, o_ref,
    kv, anc, qt, acc, mst, kc, vc, sb, pb, mb, shrink,
    rs, ss, zs, ars, ass,
):
    me = lax.axis_index("seq")
    z = me // PLANE
    x = (me % PLANE) // NY
    y = me % NY
    npairs = z // 2 + 1

    def seq_of(zz, xx, yy):
        return zz * PLANE + xx * NY + yy

    xp, xm, x2 = (x + 1) % NX, (x + NX - 1) % NX, (x + 2) % NX
    yp, ym, y2 = (y + 1) % NY, (y + NY - 1) % NY, (y + 2) % NY
    plus = {0: seq_of(z, x, yp), 1: seq_of(z, xp, y)}
    minus = {0: seq_of(z, x, ym), 1: seq_of(z, xm, y)}

    def remote(src, dst, send_sem, recv_sem, target):
        return pltpu.make_async_remote_copy(
            src_ref=src, dst_ref=dst, send_sem=send_sem, recv_sem=recv_sem,
            device_id={"seq": target}, device_id_type=pl.DeviceIdType.MESH,
        )

    barrier = pltpu.get_barrier_semaphore()
    for other in (plus[0], minus[0], plus[1], minus[1]):
        pl.semaphore_signal(barrier, inc=1, device_id={"seq": other}, device_id_type=pl.DeviceIdType.MESH)
    for dz in range(1, NZ):
        pl.semaphore_signal(
            barrier, inc=1, device_id={"seq": seq_of((z + dz) % NZ, x, y)}, device_id_type=pl.DeviceIdType.MESH
        )

    ksel = jnp.zeros((128, HD), F32)
    vsel = jnp.zeros((HD, 128), F32)
    tok_row = lax.broadcasted_iota(jnp.int32, (TOK, 128), 0)
    slot = lax.broadcasted_iota(jnp.int32, (1, 128), 1)
    for g in range(2):
        picks = jnp.where(slot < cnt_ref[0:1, g : g + 1], rows_ref[0, g : g + 1, :], -1)
        hot = jnp.where(tok_row == picks, 1.0, 0.0).astype(BF16)
        ksel = ksel + dot_tn(hot, k_ref[:, g * HD : (g + 1) * HD])
        vsel = vsel + dot_tn(v_ref[:, g * HD : (g + 1) * HD], hot)
    kv[z, x, y, 0:128, :] = ksel.astype(BF16)
    kv[z, x, y, 128:256, :] = vsel.astype(BF16)
    tag = jnp.where(cnt_ref[0:1, 1:2] > 0, 1.0, 0.0)
    kv[z, x, y, 256:272, :] = jnp.broadcast_to(tag, (16, 128)).astype(BF16)

    @pl.when(me == 0)
    def _():
        for g in range(2):
            anc[g, 0:128, :] = k_ref[0:128, g * HD : (g + 1) * HD]
            anc[g, 128:256, :] = v_ref[0:128, g * HD : (g + 1) * HD].T

    pl.semaphore_wait(barrier, 4 + NZ - 1)

    def lines(layer, role, at):
        return kv.at[layer, at] if role == 0 else kv.at[layer, :, at]

    def half(ref, which):
        n = len(ref.shape) - 2
        return ref.at[(slice(None),) * n + ((slice(0, 128) if which == 0 else slice(128, BLK)),)]

    own_at = {0: x, 1: y}
    minus_at = {0: xm, 1: ym}
    plus_at = {0: xp, 1: yp}
    far_at = {0: x2, 1: y2}

    def block(layer, role, at):
        return kv.at[layer, x, at] if role == 0 else kv.at[layer, at, y]

    b_own, b_minus, b_plus, b_far = {0: y, 1: x}, {0: ym, 1: xm}, {0: yp, 1: xp}, {0: y2, 1: x2}

    def zcopy(src_layer, target):
        ref = kv.at[src_layer, x, y]
        return remote(ref, ref, zs.at[target // PLANE], rs.at[src_layer, 0], target)

    def s1(layer, role, step):
        p, m = plus[role], minus[role]
        if step == 0:
            ref, target = block(layer, role, b_own[role]), p
        elif step == 1:
            ref, target = block(layer, role, b_own[role]), m
        elif step == 2:
            ref, target = half(block(layer, role, b_minus[role]), 0), p
        else:
            ref, target = half(block(layer, role, b_plus[role]), 1), m
        return remote(ref, ref, ss.at[layer, step], rs.at[layer, 1 + step], target)

    def s1_in(layer, role, step):
        if step == 0:
            ref = block(layer, role, b_minus[role])
        elif step == 1:
            ref = block(layer, role, b_plus[role])
        else:
            ref = half(block(layer, role, b_far[role]), step - 2)
        return remote(ref, ref, ss.at[layer, step], rs.at[layer, 1 + step], plus[role])

    def s2(layer, role, step):
        p, m = plus[1 - role], minus[1 - role]
        if step == 0:
            ref, target = lines(layer, role, own_at[role]), p
        elif step == 1:
            ref, target = lines(layer, role, own_at[role]), m
        elif step == 2:
            ref, target = half(lines(layer, role, minus_at[role]), 0), p
        else:
            ref, target = half(lines(layer, role, plus_at[role]), 1), m
        return remote(ref, ref, ss.at[layer, 4 + step], rs.at[layer, 5 + step], target)

    def s2_in(layer, role, step):
        if step == 0:
            ref = lines(layer, role, minus_at[role])
        elif step == 1:
            ref = lines(layer, role, plus_at[role])
        else:
            ref = half(lines(layer, role, far_at[role]), step - 2)
        return remote(ref, ref, ss.at[layer, 4 + step], rs.at[layer, 5 + step], plus[1 - role])

    def for_pair(p, guard, body):
        @pl.when(guard)
        def _():
            body(z - 2 * p, 0)

        @pl.when(jnp.logical_and(guard, z - 2 * p - 1 >= 0))
        def _():
            body(z - 2 * p - 1, 1)

    def ev0(p):
        def body(layer, role):
            @pl.when(layer < z)
            def _():
                zcopy(layer, me).wait_recv()

            s1(layer, role, 0).start()
            s1(layer, role, 1).start()

        for_pair(p, p < npairs, body)

    def ev1(p):
        def body(layer, role):
            s1_in(layer, role, 0).wait_recv()
            s1(layer, role, 2).start()
            s1_in(layer, role, 1).wait_recv()
            s1(layer, role, 3).start()

        for_pair(p, p < npairs, body)

    def ev2(p):
        def body(layer, role):
            s1_in(layer, role, 2).wait_recv()
            s1_in(layer, role, 3).wait_recv()
            s2(layer, role, 0).start()
            s2(layer, role, 1).start()

        for_pair(p, p < npairs, body)

    def ev3(p):
        def body(layer, role):
            s2_in(layer, role, 0).wait_recv()
            s2(layer, role, 2).start()
            s2_in(layer, role, 1).wait_recv()
            s2(layer, role, 3).start()

        for_pair(p, p < npairs, body)

    def ev4(p):
        def body(layer, role):
            s2_in(layer, role, 2).wait_recv()
            s2_in(layer, role, 3).wait_recv()

        for_pair(p, p < npairs, body)

    def acopy(step, target):
        return remote(anc, anc, ass.at[step], ars, target)

    in_first = x == 0
    a_root = jnp.logical_and(x == 0, y == 0)

    def anchor_in():
        acopy(0, me).wait_recv()

    @pl.loop(z + 1, NZ)
    def _(zz):
        zcopy(z, seq_of(zz, x, y)).start()

    ev0(0)

    @pl.when(me == 0)
    def _():
        for zz in range(1, NZ):
            acopy(zz - 1, seq_of(zz, 0, 0)).start()

    for j in range(8):
        for g in range(2):
            h = g * 8 + j
            qt[j // 4, g * HD : (g + 1) * HD, (j % 4) * TOK : (j % 4 + 1) * TOK] = q_ref[:, h * HD : (h + 1) * HD].T

    def simple_chunk(nb, causal):
        for r in range(NR):
            s = dot(kc[0, 0 : nb * 128], qt[r])
            if causal:
                key_tok = lax.broadcasted_iota(jnp.int32, (TOK, TOK), 0)
                query_tok = lax.broadcasted_iota(jnp.int32, (TOK, TOK), 1)
                bias = jnp.where(key_tok <= query_tok, 0.0, LOW)
                bias = jnp.concatenate([bias] * (R // TOK), axis=1)
                s = s + jnp.concatenate([bias] * 2, axis=0)
            sb[r, 0 : nb * 128] = s
            hb = nb * 64
            for g in range(2):
                old = mst[r, g : g + 1]
                new = jnp.maximum(old, jnp.max(s[g * hb : (g + 1) * hb], axis=0, keepdims=True))
                mst[r, g : g + 1] = new
                shrink[0, r, g : g + 1] = jnp.exp2((old - new) * CSC)
                pb[r, g * hb : (g + 1) * hb] = jnp.exp2((sb[r, g * hb : (g + 1) * hb] - new) * CSC).astype(BF16)
            accumulate(0, r, dot(vc[0, :, 0 : nb * 128], pb[r, 0 : nb * 128]))

    def accumulate(par, r, d):
        a0 = shrink[par, r, 0:1]
        a1 = shrink[par, r, 1:2]
        acc[r, 0:128] = acc[r, 0:128] * a0 + d[0:128]
        acc[r, 128:256] = acc[r, 128:256] * a1 + d[128:256]
        acc[r, 256:257] = acc[r, 256:257] * a0 + d[256:257]
        acc[r, 257:258] = acc[r, 257:258] * a1 + d[257:258]

    tag_row = lax.broadcasted_iota(jnp.int32, (16, 128), 0)

    def put_block(par, j, keys, vals, m0, m1):
        cols = slice(j * 128, (j + 1) * 128)
        zero = jnp.zeros((128, 128), BF16)
        kc[par, cols, 0:128] = jnp.where(m0 > 0, keys, zero)
        kc[par, cols, 128:256] = jnp.where(m1 > 0, keys, zero)
        vc[par, 0:128, cols] = jnp.where(m0 > 0, vals, zero)
        vc[par, 128:256, cols] = jnp.where(m1 > 0, vals, zero)
        ones = jnp.where(tag_row == 0, m0, jnp.where(tag_row == 1, m1, 0.0))
        vc[par, 256:272, cols] = ones.astype(BF16)

    one_row = jnp.ones((1, 128), F32)
    zero_row = jnp.zeros((1, 128), F32)

    acc[...] = jnp.zeros_like(acc)
    mst[...] = jnp.full_like(mst, LOW)
    for g in range(2):
        vt = v_ref[:, g * HD : (g + 1) * HD].T
        for i in range(2):
            put_block(
                0, 2 * g + i, k_ref[i * 128 : (i + 1) * 128, g * HD : (g + 1) * HD], vt[:, i * 128 : (i + 1) * 128],
                one_row if g == 0 else zero_row, one_row if g == 1 else zero_row,
            )
    simple_chunk(4, True)

    def blocks_of(chunk):
        out = []
        for layer, role, at in chunk:
            for i in range(4):
                bx, by = (at, i) if role == 0 else (i, at)
                ok = jnp.minimum(layer + 1, 1)
                out.append((ok * layer + (1 - ok) * z, ok * bx + (1 - ok) * x, ok * by + (1 - ok) * y))
        return out

    def masks(layer, bx, by):
        seen = jnp.where(layer * PLANE + bx * NY + by < me, 1.0, 0.0)
        t = kv[layer, bx, by, 256:272, :].astype(F32)[0:1]
        m1 = t * seen
        m0 = seen - m1
        return m0, m1

    def expand(chunk, par):
        for j, (layer, bx, by) in enumerate(blocks_of(chunk)):
            m0, m1 = masks(layer, bx, by)
            put_block(par, j, kv[layer, bx, by, 0:128, :], kv[layer, bx, by, 128:256, :], m0, m1)

    def score(chunk, par, r):
        s = dot(kc[par], qt[r])
        sb[r] = s
        m0o, m1o = mst[r, 0:1], mst[r, 1:2]
        m0, m1 = m0o, m1o
        ms = []
        for j, (layer, bx, by) in enumerate(blocks_of(chunk)):
            k0, k1 = masks(layer, bx, by)
            k0, k1 = widen(k0) > 0, widen(k1) > 0
            ms.append((k0, k1))
            top = jnp.max(s[j * 128 : (j + 1) * 128], axis=0, keepdims=True)
            m0 = jnp.maximum(m0, jnp.where(k0, top, LOW))
            m1 = jnp.maximum(m1, jnp.where(k1, top, LOW))
        mst[r, 0:1] = m0
        mst[r, 1:2] = m1
        for j, (k0, k1) in enumerate(ms):
            mb[r, j : j + 1] = jnp.where(k0, m0, jnp.where(k1, m1, HIGH))
        shrink[par, r, 0:1] = jnp.exp2((m0o - m0) * CSC)
        shrink[par, r, 1:2] = jnp.exp2((m1o - m1) * CSC)

    def weigh(r):
        for j in range(CB):
            rows = slice(j * 128, (j + 1) * 128)
            pb[r, rows] = jnp.exp2((sb[r, rows] - mb[r, j : j + 1]) * CSC).astype(BF16)

    def absorb(par, r):
        accumulate(par, r, dot(vc[par], pb[r]))

    def run_chunk(cur, nxt, par, between):
        score(cur, par, 1)
        absorb(1 - par, 1)
        weigh(0)
        between()
        expand(nxt, 1 - par)
        score(nxt, 1 - par, 0)
        absorb(par, 0)
        weigh(1)

    def chunk_a(p):
        return ((z - 2 * p, 0, x), (z - 2 * p - 1, 1, y))

    def chunk_b(p, k):
        la, lb = z - 2 * p, z - 2 * p - 1
        if k == 0:
            return ((la, 0, xm), (la, 0, xp))
        if k == 1:
            return ((lb, 1, ym), (lb, 1, yp))
        return ((la, 0, x2), (lb, 1, y2))

    def comm_a(i):
        ev0(i)
        ev1(i - 1)
        ev2(i - 2)

    ev0(1)
    ev1(0)
    ev0(2)
    ev1(1)
    ev2(0)

    @pl.when(a_root)
    def _():
        @pl.when(z > 0)
        def _():
            anchor_in()

        acopy(7, seq_of(z, 0, 1)).start()
        acopy(8, seq_of(z, 0, 3)).start()

    pb[1] = jnp.zeros_like(pb[1])
    vc[1] = jnp.zeros_like(vc[1])
    shrink[1] = jnp.ones_like(shrink[1])
    expand(chunk_a(0), 0)
    score(chunk_a(0), 0, 0)

    @pl.loop(0, npairs - 1)
    def _(p):
        run_chunk(chunk_a(p), chunk_a(p + 1), lax.rem(p, 2), functools.partial(comm_a, p + 3))

    run_chunk(chunk_a(npairs - 1), chunk_b(0, 0), lax.rem(npairs - 1, 2), functools.partial(ev3, 0))

    @pl.when(jnp.logical_and(in_first, y > 0))
    def _():
        anchor_in()

    @pl.when(jnp.logical_and(in_first, y == 1))
    def _():
        acopy(7, seq_of(z, 0, 2)).start()

    @pl.when(in_first)
    def _():
        acopy(9, seq_of(z, 1, y)).start()
        acopy(10, seq_of(z, 3, y)).start()

    @pl.loop(0, npairs)
    def _(p):
        par = lax.rem(npairs + 3 * p, 2)
        nxt = jnp.minimum(p + 1, npairs - 1)
        run_chunk(chunk_b(p, 0), chunk_b(p, 1), par, lambda: None)
        run_chunk(chunk_b(p, 1), chunk_b(p, 2), 1 - par, functools.partial(ev4, p))
        run_chunk(chunk_b(p, 2), chunk_b(nxt, 0), par, functools.partial(ev3, p + 1))

    absorb(1 - lax.rem(npairs * 4, 2), 1)

    @pl.when(x > 0)
    def _():
        anchor_in()

    @pl.when(x == 1)
    def _():
        acopy(9, seq_of(z, 2, y)).start()

    @pl.when(me > 0)
    def _():
        for g in range(2):
            put_block(
                0, g, anc[g, 0:128, :], anc[g, 128:256, :],
                one_row if g == 0 else zero_row, one_row if g == 1 else zero_row,
            )
        simple_chunk(2, False)

    for j in range(8):
        cols = slice((j % 4) * TOK, (j % 4 + 1) * TOK)
        for g in range(2):
            h = g * 8 + j
            total = acc[j // 4, 256 + g : 257 + g, cols]
            mixed = acc[j // 4, g * HD : (g + 1) * HD, cols] / total
            o_ref[:, h * HD : (h + 1) * HD] = mixed.astype(BF16).T

    @pl.loop(z + 1, NZ)
    def _(zz):
        zcopy(z, seq_of(zz, x, y)).wait_send()

    def drain(p):
        def body(layer, role):
            for step in range(4):
                s1(layer, role, step).wait_send()
                s2(layer, role, step).wait_send()

        for_pair(p, p < npairs, body)

    @pl.loop(0, npairs)
    def _(p):
        drain(p)

    @pl.when(me == 0)
    def _():
        for zz in range(1, NZ):
            acopy(zz - 1, me).wait_send()

    @pl.when(a_root)
    def _():
        acopy(7, me).wait_send()
        acopy(8, me).wait_send()

    @pl.when(jnp.logical_and(in_first, y == 1))
    def _():
        acopy(7, me).wait_send()

    @pl.when(in_first)
    def _():
        acopy(9, me).wait_send()
        acopy(10, me).wait_send()

    @pl.when(x == 1)
    def _():
        acopy(9, me).wait_send()


def per_device(queries, keys, values, kept_count, kept_rows):
    vmem = pl.BlockSpec(memory_space=pltpu.VMEM)
    return pl.pallas_call(
        kernel,
        out_shape=jax.ShapeDtypeStruct(queries.shape, BF16),
        in_specs=[vmem] * 5,
        out_specs=vmem,
        scratch_shapes=[
            pltpu.VMEM((NZ, NX, NY, BLK, 128), BF16),
            pltpu.VMEM((2, 256, 128), BF16),
            pltpu.VMEM((NR, 2 * HD, R), BF16),
            pltpu.VMEM((NR, BLK, R), F32),
            pltpu.VMEM((NR, 8, R), F32),
            pltpu.VMEM((2, NK, 2 * HD), BF16),
            pltpu.VMEM((2, BLK, NK), BF16),
            pltpu.VMEM((NR, NK, R), F32),
            pltpu.VMEM((NR, NK, R), BF16),
            pltpu.VMEM((NR, CB, R), F32),
            pltpu.VMEM((2, NR, 8, R), F32),
            pltpu.SemaphoreType.DMA((NZ, 9)),
            pltpu.SemaphoreType.DMA((NZ, 8)),
            pltpu.SemaphoreType.DMA((NZ,)),
            pltpu.SemaphoreType.DMA,
            pltpu.SemaphoreType.DMA((11,)),
        ],
        compiler_params=pltpu.CompilerParams(
            collective_id=0, has_side_effects=True, vmem_limit_bytes=56 * 2**20
        ),
        cost_estimate=pl.CostEstimate(flops=17_000_000_000, bytes_accessed=4_000_000, transcendentals=33_000_000),
    )(queries, keys, values, kept_count, kept_rows)


def solution(mesh):
    return jax.shard_map(
        per_device,
        mesh=mesh,
        in_specs=(
            P("seq", "head"),
            P("seq", "head"),
            P("seq", "head"),
            P("seq", "head"),
            P("seq", "head", None),
        ),
        out_specs=P("seq", "head"),
        check_vma=False,
    )
```

time: 569 us -> 101 us (0.18); the launches traced: 558 us -> 101 us
  waiting for transfers between devices: 287 us -> 0 us
  Pallas kernels: 0 us -> 98.3 us
  local copies, waits for them, and re-layouts: 88.7 us -> 2.3 us
  matrix products: 84.9 us -> 0 us
  other arithmetic: 57.7 us -> 0 us
  blocking collectives: 21.3 us -> 0 us
  between operations: 16.6 us -> 0.01 us
    psum x1 -> x0, waiting for transfers between devices: 169 us -> none  [from_root(): return lax.psum(kept, axis)]
    all_gather x1 -> x0, waiting for transfers between devices: 119 us -> none  [per_device(): lax.all_gather(own_block, 'seq', axis=0, tiled=True)]
    pallas_call x0 -> x1, Pallas kernels: none -> 98.3 us  [per_device(): pl.pallas_call(kernel, out_shape=jax.ShapeDtypeStruct(queries.shape, BF16...]
    dot_general x36 -> x0, matrix products: 84.9 us -> none  [the longest x17 59.5 us: absorb(): jnp.einsum(form, weights.astype(jnp.bfloat16), value_rows, preferred_elem...]
    gather x18 -> x0, local copies, waits for them, and re-layouts: 66 us -> none  [the longest x16 64.6 us: visit(): chosen = every_block[picks]]
    reduce_sum x19 -> x0, other arithmetic: 38.8 us -> none  [the longest x17 36.6 us: absorb(): run_total = run_total * shrink + jnp.sum(weights, axis=-1)]
    unnamed x1 -> x0, blocking collectives: 21.3 us -> none
    lt x16 -> x0, other arithmetic: 9.36 us -> none  [visit(): turn * hosts_per_turn + jnp.arange(hosts_per_turn, dtype=jnp.int32)]
  transfers between devices with their start and end apart: 2 -> 0, of which waited for: 2 -> 0; matrix products, arithmetic and copies ran while one was open for 5% -> 0% of each run, Pallas kernels for 0% -> 0%
where the time goes in v1:
time: 101 us
  Pallas kernels  98.3 us (97%)
  local copies, waits for them, and re-layouts  2.3 us (2%)
    pallas_call x1, Pallas kernels, per_device(): pl.pallas_call(kernel, out_shape=jax.ShapeDtypeStruct(queries.shape, BF16...  98.3 us
    unnamed x1, local copies, waits for them, and re-layouts  2.3 us

profile of v1, /device:TPU:228, one launch (start us, length us, event | category | flops | bytes accessed | tf_op | source)
XLA Modules:
  0.0 100.6 jit_solution(15227928905953395269)
XLA Ops:
  0.0 98.3 %shard_map.55 = bf16[256,2048]{1,0:T(8,128)(2,1)} custom-call(bf16[256,2048]{1,0:T(8,128)(2,1)} %q_ref.1, bf16[256,256]{1,0:T(8,128)(2,1)} %k_ref.1, bf16[256,256]{1,0:T(8,128)(2,1)} %v_ref.1, s32[1,2]{1,0:T(1,128)} %cnt_ref.1, s32[1,2,128]{2,1,0:T(2,128)} %rows_ref.1), custom_call_target="tpu_custom_call" | custom-call | flops 16999999488 | bytes 4000000 | tf_op jit(solution)/shard_map/pallas_call | solution.py:481
  98.3 2.3 %copy.7 = bf16[256,2048]{1,0:T(8,128)(2,1)} copy(bf16[256,2048]{1,0:T(8,128)(2,1)} %shard_map.55) | data formatting | bytes 2097152

commit v2 on v1

--- a/solution.py
+++ b/solution.py
@@ -38,7 +38,7 @@
 
 def kernel(
     q_ref, k_ref, v_ref, cnt_ref, rows_ref, o_ref,
-    kv, anc, qt, acc, mst, kc, vc, sb, pb, mb, shrink,
+    kv, anc, qt, acc, mst, kc, vc, sb, pb, mb, shrink, msk,
     rs, ss, zs, ars, ass,
 ):
     me = lax.axis_index("seq")
@@ -54,6 +54,7 @@
     yp, ym, y2 = (y + 1) % NY, (y + NY - 1) % NY, (y + 2) % NY
     plus = {0: seq_of(z, x, yp), 1: seq_of(z, xp, y)}
     minus = {0: seq_of(z, x, ym), 1: seq_of(z, xm, y)}
+    far = {0: seq_of(z, x, y2), 1: seq_of(z, x2, y)}
 
     def remote(src, dst, send_sem, recv_sem, target):
         return pltpu.make_async_remote_copy(
@@ -62,7 +63,7 @@
         )
 
     barrier = pltpu.get_barrier_semaphore()
-    for other in (plus[0], minus[0], plus[1], minus[1]):
+    for other in (plus[0], minus[0], far[0], plus[1], minus[1], far[1]):
         pl.semaphore_signal(barrier, inc=1, device_id={"seq": other}, device_id_type=pl.DeviceIdType.MESH)
     for dz in range(1, NZ):
         pl.semaphore_signal(
@@ -89,14 +90,13 @@
             anc[g, 0:128, :] = k_ref[0:128, g * HD : (g + 1) * HD]
             anc[g, 128:256, :] = v_ref[0:128, g * HD : (g + 1) * HD].T
 
-    pl.semaphore_wait(barrier, 4 + NZ - 1)
+    pl.semaphore_wait(barrier, 6 + NZ - 1)
 
     def lines(layer, role, at):
         return kv.at[layer, at] if role == 0 else kv.at[layer, :, at]
 
     def half(ref, which):
-        n = len(ref.shape) - 2
-        return ref.at[(slice(None),) * n + ((slice(0, 128) if which == 0 else slice(128, BLK)),)]
+        return ref.at[:, 0:128] if which == 0 else ref.at[:, 128:BLK]
 
     own_at = {0: x, 1: y}
     minus_at = {0: xm, 1: ym}
@@ -113,46 +113,30 @@
         return remote(ref, ref, zs.at[target // PLANE], rs.at[src_layer, 0], target)
 
     def s1(layer, role, step):
-        p, m = plus[role], minus[role]
-        if step == 0:
-            ref, target = block(layer, role, b_own[role]), p
-        elif step == 1:
-            ref, target = block(layer, role, b_own[role]), m
-        elif step == 2:
-            ref, target = half(block(layer, role, b_minus[role]), 0), p
-        else:
-            ref, target = half(block(layer, role, b_plus[role]), 1), m
+        ref = block(layer, role, b_own[role])
+        target = (plus, minus, far)[step][role]
         return remote(ref, ref, ss.at[layer, step], rs.at[layer, 1 + step], target)
 
     def s1_in(layer, role, step):
-        if step == 0:
-            ref = block(layer, role, b_minus[role])
-        elif step == 1:
-            ref = block(layer, role, b_plus[role])
-        else:
-            ref = half(block(layer, role, b_far[role]), step - 2)
+        ref = block(layer, role, (b_minus, b_plus, b_far)[step][role])
         return remote(ref, ref, ss.at[layer, step], rs.at[layer, 1 + step], plus[role])
 
     def s2(layer, role, step):
         p, m = plus[1 - role], minus[1 - role]
-        if step == 0:
-            ref, target = lines(layer, role, own_at[role]), p
-        elif step == 1:
-            ref, target = lines(layer, role, own_at[role]), m
+        if step < 2:
+            ref, target = lines(layer, role, own_at[role]), (p, m)[step]
         elif step == 2:
             ref, target = half(lines(layer, role, minus_at[role]), 0), p
         else:
             ref, target = half(lines(layer, role, plus_at[role]), 1), m
-        return remote(ref, ref, ss.at[layer, 4 + step], rs.at[layer, 5 + step], target)
+        return remote(ref, ref, ss.at[layer, 3 + step], rs.at[layer, 4 + step], target)
 
     def s2_in(layer, role, step):
-        if step == 0:
-            ref = lines(layer, role, minus_at[role])
-        elif step == 1:
-            ref = lines(layer, role, plus_at[role])
+        if step < 2:
+            ref = lines(layer, role, (minus_at, plus_at)[step][role])
         else:
             ref = half(lines(layer, role, far_at[role]), step - 2)
-        return remote(ref, ref, ss.at[layer, 4 + step], rs.at[layer, 5 + step], plus[1 - role])
+        return remote(ref, ref, ss.at[layer, 3 + step], rs.at[layer, 4 + step], plus[1 - role])
 
     def for_pair(p, guard, body):
         @pl.when(guard)
@@ -168,25 +152,24 @@
             @pl.when(layer < z)
             def _():
                 zcopy(layer, me).wait_recv()
-
-            s1(layer, role, 0).start()
-            s1(layer, role, 1).start()
+                for step in range(3):
+                    s1(layer, role, step).start()
 
         for_pair(p, p < npairs, body)
 
     def ev1(p):
         def body(layer, role):
-            s1_in(layer, role, 0).wait_recv()
-            s1(layer, role, 2).start()
-            s1_in(layer, role, 1).wait_recv()
-            s1(layer, role, 3).start()
+            for step in range(3):
+                s1_in(layer, role, step).wait_recv()
 
         for_pair(p, p < npairs, body)
 
-    def ev2(p):
+        @pl.when(p <= 0)
+        def _():
+            lines_out(p)
+
+    def lines_out(p):
         def body(layer, role):
-            s1_in(layer, role, 2).wait_recv()
-            s1_in(layer, role, 3).wait_recv()
             s2(layer, role, 0).start()
             s2(layer, role, 1).start()
 
@@ -200,6 +183,7 @@
             s2(layer, role, 3).start()
 
         for_pair(p, p < npairs, body)
+        lines_out(p + 1)
 
     def ev4(p):
         def body(layer, role):
@@ -217,16 +201,12 @@
     def anchor_in():
         acopy(0, me).wait_recv()
 
+    for step in range(3):
+        s1(z, 0, step).start()
+
     @pl.loop(z + 1, NZ)
     def _(zz):
         zcopy(z, seq_of(zz, x, y)).start()
-
-    ev0(0)
-
-    @pl.when(me == 0)
-    def _():
-        for zz in range(1, NZ):
-            acopy(zz - 1, seq_of(zz, 0, 0)).start()
 
     for j in range(8):
         for g in range(2):
@@ -305,17 +285,18 @@
     def expand(chunk, par):
         for j, (layer, bx, by) in enumerate(blocks_of(chunk)):
             m0, m1 = masks(layer, bx, by)
+            msk[par, j : j + 1] = m0
+            msk[par, CB + j : CB + j + 1] = m1
             put_block(par, j, kv[layer, bx, by, 0:128, :], kv[layer, bx, by, 128:256, :], m0, m1)
 
-    def score(chunk, par, r):
+    def score(par, r):
         s = dot(kc[par], qt[r])
         sb[r] = s
         m0o, m1o = mst[r, 0:1], mst[r, 1:2]
         m0, m1 = m0o, m1o
         ms = []
-        for j, (layer, bx, by) in enumerate(blocks_of(chunk)):
-            k0, k1 = masks(layer, bx, by)
-            k0, k1 = widen(k0) > 0, widen(k1) > 0
+        for j in range(CB):
+            k0, k1 = widen(msk[par, j : j + 1]) > 0, widen(msk[par, CB + j : CB + j + 1]) > 0
             ms.append((k0, k1))
             top = jnp.max(s[j * 128 : (j + 1) * 128], axis=0, keepdims=True)
             m0 = jnp.maximum(m0, jnp.where(k0, top, LOW))
@@ -335,13 +316,13 @@
     def absorb(par, r):
         accumulate(par, r, dot(vc[par], pb[r]))
 
-    def run_chunk(cur, nxt, par, between):
-        score(cur, par, 1)
+    def run_chunk(nxt, par, between):
+        score(par, 1)
         absorb(1 - par, 1)
         weigh(0)
         between()
         expand(nxt, 1 - par)
-        score(nxt, 1 - par, 0)
+        score(1 - par, 0)
         absorb(par, 0)
         weigh(1)
 
@@ -359,65 +340,73 @@
     def comm_a(i):
         ev0(i)
         ev1(i - 1)
-        ev2(i - 2)
-
+
+    ev0(0)
+    ev1(0)
     ev0(1)
-    ev1(0)
-    ev0(2)
-    ev1(1)
-    ev2(0)
-
-    @pl.when(a_root)
-    def _():
-        @pl.when(z > 0)
+
+    @pl.when(me == 0)
+    def _():
+        for zz in range(1, NZ):
+            acopy(zz - 1, seq_of(zz, 0, 0)).start()
+
+    def anchor_along_y():
+        @pl.when(a_root)
         def _():
-            anchor_in()
-
-        acopy(7, seq_of(z, 0, 1)).start()
-        acopy(8, seq_of(z, 0, 3)).start()
+            @pl.when(z > 0)
+            def _():
+                anchor_in()
+
+            for i in range(3):
+                acopy(7 + i, seq_of(z, 0, i + 1)).start()
+
+    def anchor_along_x():
+        @pl.when(in_first)
+        def _():
+            @pl.when(y > 0)
+            def _():
+                anchor_in()
+
+            for i in range(3):
+                acopy(10 + i, seq_of(z, i + 1, y)).start()
 
     pb[1] = jnp.zeros_like(pb[1])
     vc[1] = jnp.zeros_like(vc[1])
     shrink[1] = jnp.ones_like(shrink[1])
     expand(chunk_a(0), 0)
-    score(chunk_a(0), 0, 0)
+    score(0, 0)
 
     @pl.loop(0, npairs - 1)
     def _(p):
-        run_chunk(chunk_a(p), chunk_a(p + 1), lax.rem(p, 2), functools.partial(comm_a, p + 3))
-
-    run_chunk(chunk_a(npairs - 1), chunk_b(0, 0), lax.rem(npairs - 1, 2), functools.partial(ev3, 0))
-
-    @pl.when(jnp.logical_and(in_first, y > 0))
-    def _():
-        anchor_in()
-
-    @pl.when(jnp.logical_and(in_first, y == 1))
-    def _():
-        acopy(7, seq_of(z, 0, 2)).start()
-
-    @pl.when(in_first)
-    def _():
-        acopy(9, seq_of(z, 1, y)).start()
-        acopy(10, seq_of(z, 3, y)).start()
+        run_chunk(chunk_a(p + 1), lax.rem(p, 2), functools.partial(comm_a, p + 2))
+
+    run_chunk(chunk_b(0, 0), lax.rem(npairs - 1, 2), functools.partial(ev3, 0))
 
     @pl.loop(0, npairs)
     def _(p):
         par = lax.rem(npairs + 3 * p, 2)
-        nxt = jnp.minimum(p + 1, npairs - 1)
-        run_chunk(chunk_b(p, 0), chunk_b(p, 1), par, lambda: None)
-        run_chunk(chunk_b(p, 1), chunk_b(p, 2), 1 - par, functools.partial(ev4, p))
-        run_chunk(chunk_b(p, 2), chunk_b(nxt, 0), par, functools.partial(ev3, p + 1))
+
+        def near():
+            @pl.when(p == 0)
+            def _():
+                anchor_along_y()
+
+        def away():
+            ev4(p)
+
+            @pl.when(p == jnp.minimum(1, npairs - 1))
+            def _():
+                anchor_along_x()
+
+        run_chunk(chunk_b(p, 1), par, near)
+        run_chunk(chunk_b(p, 2), 1 - par, away)
+        run_chunk(chunk_b(jnp.minimum(p + 1, npairs - 1), 0), par, functools.partial(ev3, p + 1))
 
     absorb(1 - lax.rem(npairs * 4, 2), 1)
 
     @pl.when(x > 0)
     def _():
         anchor_in()
-
-    @pl.when(x == 1)
-    def _():
-        acopy(9, seq_of(z, 2, y)).start()
 
     @pl.when(me > 0)
     def _():
@@ -442,8 +431,9 @@
 
     def drain(p):
         def body(layer, role):
+            for step in range(3):
+                s1(layer, role, step).wait_send()
             for step in range(4):
-                s1(layer, role, step).wait_send()
                 s2(layer, role, step).wait_send()
 
         for_pair(p, p < npairs, body)
@@ -459,21 +449,13 @@
 
     @pl.when(a_root)
     def _():
-        acopy(7, me).wait_send()
-        acopy(8, me).wait_send()
-
-    @pl.when(jnp.logical_and(in_first, y == 1))
-    def _():
-        acopy(7, me).wait_send()
+        for i in range(3):
+            acopy(7 + i, me).wait_send()
 
     @pl.when(in_first)
     def _():
-        acopy(9, me).wait_send()
-        acopy(10, me).wait_send()
-
-    @pl.when(x == 1)
-    def _():
-        acopy(9, me).wait_send()
+        for i in range(3):
+            acopy(10 + i, me).wait_send()
 
 
 def per_device(queries, keys, values, kept_count, kept_rows):
@@ -495,11 +477,12 @@
             pltpu.VMEM((NR, NK, R), BF16),
             pltpu.VMEM((NR, CB, R), F32),
             pltpu.VMEM((2, NR, 8, R), F32),
-            pltpu.SemaphoreType.DMA((NZ, 9)),
+            pltpu.VMEM((2, 2 * CB, 128), F32),
+            pltpu.SemaphoreType.DMA((NZ, 8)),
             pltpu.SemaphoreType.DMA((NZ, 8)),
             pltpu.SemaphoreType.DMA((NZ,)),
             pltpu.SemaphoreType.DMA,
-            pltpu.SemaphoreType.DMA((11,)),
+            pltpu.SemaphoreType.DMA((13,)),
         ],
         compiler_params=pltpu.CompilerParams(
             collective_id=0, has_side_effects=True, vmem_limit_bytes=56 * 2**20

time: 101 us -> 90.7 us (0.90)
  the two profiles are of different devices: /device:TPU:228 before, /device:TPU:194 now
where the time goes in v2:
time: 90.7 us; the launch traced here: 90.6 us
  Pallas kernels  88.2 us (97%)
  local copies, waits for them, and re-layouts  2.3 us (3%)
    pallas_call x1, Pallas kernels, per_device(): pl.pallas_call(kernel, out_shape=jax.ShapeDtypeStruct(queries.shape, BF16...  88.2 us
    unnamed x1, local copies, waits for them, and re-layouts  2.3 us

profile of v2, /device:TPU:194, one launch (start us, length us, event | category | flops | bytes accessed | tf_op | source)
XLA Modules:
  0.0 90.6 jit_solution(365234274216297677)
XLA Ops:
  0.0 88.2 %shard_map.55 = bf16[256,2048]{1,0:T(8,128)(2,1)} custom-call(bf16[256,2048]{1,0:T(8,128)(2,1)} %q_ref.1, bf16[256,256]{1,0:T(8,128)(2,1)} %k_ref.1, bf16[256,256]{1,0:T(8,128)(2,1)} %v_ref.1, s32[1,2]{1,0:T(1,128)} %cnt_ref.1, s32[1,2,128]{2,1,0:T(2,128)} %rows_ref.1), custom_call_target="tpu_custom_call" | custom-call | flops 16999999488 | bytes 4000000 | tf_op jit(solution)/shard_map/pallas_call | solution.py:463
  88.2 2.3 %copy.7 = bf16[256,2048]{1,0:T(8,128)(2,1)} copy(bf16[256,2048]{1,0:T(8,128)(2,1)} %shard_map.55) | data formatting | bytes 2097152

commit v3 on v2

--- a/solution.py
+++ b/solution.py
@@ -38,7 +38,7 @@
 
 def kernel(
     q_ref, k_ref, v_ref, cnt_ref, rows_ref, o_ref,
-    kv, anc, qt, acc, mst, kc, vc, sb, pb, mb, shrink, msk,
+    kv, anc, qt, acc, mst, kc, vc, sb, pb, mb, shrink, msk, tot,
     rs, ss, zs, ars, ass,
 ):
     me = lax.axis_index("seq")
@@ -229,7 +229,9 @@
                 new = jnp.maximum(old, jnp.max(s[g * hb : (g + 1) * hb], axis=0, keepdims=True))
                 mst[r, g : g + 1] = new
                 shrink[0, r, g : g + 1] = jnp.exp2((old - new) * CSC)
-                pb[r, g * hb : (g + 1) * hb] = jnp.exp2((sb[r, g * hb : (g + 1) * hb] - new) * CSC).astype(BF16)
+                w = jnp.exp2((sb[r, g * hb : (g + 1) * hb] - new) * CSC)
+                pb[r, g * hb : (g + 1) * hb] = w.astype(BF16)
+                tot[r, g : g + 1] = tot[r, g : g + 1] * shrink[0, r, g : g + 1] + jnp.sum(w, axis=0, keepdims=True)
             accumulate(0, r, dot(vc[0, :, 0 : nb * 128], pb[r, 0 : nb * 128]))
 
     def accumulate(par, r, d):
@@ -237,10 +239,6 @@
         a1 = shrink[par, r, 1:2]
         acc[r, 0:128] = acc[r, 0:128] * a0 + d[0:128]
         acc[r, 128:256] = acc[r, 128:256] * a1 + d[128:256]
-        acc[r, 256:257] = acc[r, 256:257] * a0 + d[256:257]
-        acc[r, 257:258] = acc[r, 257:258] * a1 + d[257:258]
-
-    tag_row = lax.broadcasted_iota(jnp.int32, (16, 128), 0)
 
     def put_block(par, j, keys, vals, m0, m1):
         cols = slice(j * 128, (j + 1) * 128)
@@ -249,13 +247,12 @@
         kc[par, cols, 128:256] = jnp.where(m1 > 0, keys, zero)
         vc[par, 0:128, cols] = jnp.where(m0 > 0, vals, zero)
         vc[par, 128:256, cols] = jnp.where(m1 > 0, vals, zero)
-        ones = jnp.where(tag_row == 0, m0, jnp.where(tag_row == 1, m1, 0.0))
-        vc[par, 256:272, cols] = ones.astype(BF16)
 
     one_row = jnp.ones((1, 128), F32)
     zero_row = jnp.zeros((1, 128), F32)
 
     acc[...] = jnp.zeros_like(acc)
+    tot[...] = jnp.zeros_like(tot)
     mst[...] = jnp.full_like(mst, LOW)
     for g in range(2):
         vt = v_ref[:, g * HD : (g + 1) * HD].T
@@ -308,10 +305,18 @@
         shrink[par, r, 0:1] = jnp.exp2((m0o - m0) * CSC)
         shrink[par, r, 1:2] = jnp.exp2((m1o - m1) * CSC)
 
-    def weigh(r):
+    def weigh(par, r):
+        t0 = tot[r, 0:1] * shrink[par, r, 0:1]
+        t1 = tot[r, 1:2] * shrink[par, r, 1:2]
         for j in range(CB):
             rows = slice(j * 128, (j + 1) * 128)
-            pb[r, rows] = jnp.exp2((sb[r, rows] - mb[r, j : j + 1]) * CSC).astype(BF16)
+            w = jnp.exp2((sb[r, rows] - mb[r, j : j + 1]) * CSC)
+            pb[r, rows] = w.astype(BF16)
+            part = jnp.sum(w, axis=0, keepdims=True)
+            t0 = t0 + part * widen(msk[par, j : j + 1])
+            t1 = t1 + part * widen(msk[par, CB + j : CB + j + 1])
+        tot[r, 0:1] = t0
+        tot[r, 1:2] = t1
 
     def absorb(par, r):
         accumulate(par, r, dot(vc[par], pb[r]))
@@ -319,12 +324,12 @@
     def run_chunk(nxt, par, between):
         score(par, 1)
         absorb(1 - par, 1)
-        weigh(0)
+        weigh(par, 0)
         between()
         expand(nxt, 1 - par)
         score(1 - par, 0)
         absorb(par, 0)
-        weigh(1)
+        weigh(par, 1)
 
     def chunk_a(p):
         return ((z - 2 * p, 0, x), (z - 2 * p - 1, 1, y))
@@ -421,7 +426,7 @@
         cols = slice((j % 4) * TOK, (j % 4 + 1) * TOK)
         for g in range(2):
             h = g * 8 + j
-            total = acc[j // 4, 256 + g : 257 + g, cols]
+            total = tot[j // 4, g : g + 1, cols]
             mixed = acc[j // 4, g * HD : (g + 1) * HD, cols] / total
             o_ref[:, h * HD : (h + 1) * HD] = mixed.astype(BF16).T
 
@@ -469,15 +474,16 @@
             pltpu.VMEM((NZ, NX, NY, BLK, 128), BF16),
             pltpu.VMEM((2, 256, 128), BF16),
             pltpu.VMEM((NR, 2 * HD, R), BF16),
-            pltpu.VMEM((NR, BLK, R), F32),
+            pltpu.VMEM((NR, 2 * HD, R), F32),
             pltpu.VMEM((NR, 8, R), F32),
             pltpu.VMEM((2, NK, 2 * HD), BF16),
-            pltpu.VMEM((2, BLK, NK), BF16),
+            pltpu.VMEM((2, 2 * HD, NK), BF16),
             pltpu.VMEM((NR, NK, R), F32),
             pltpu.VMEM((NR, NK, R), BF16),
             pltpu.VMEM((NR, CB, R), F32),
             pltpu.VMEM((2, NR, 8, R), F32),
             pltpu.VMEM((2, 2 * CB, 128), F32),
+            pltpu.VMEM((NR, 8, R), F32),
             pltpu.SemaphoreType.DMA((NZ, 8)),
             pltpu.SemaphoreType.DMA((NZ, 8)),
             pltpu.SemaphoreType.DMA((NZ,)),

time: 90.7 us -> 97.4 us (1.074)
  the two profiles are of different devices: /device:TPU:194 before, /device:TPU:192 now
where the time goes in v3:
time: 97.4 us; the launch traced here: 97.3 us
  Pallas kernels  95 us (98%)
  local copies, waits for them, and re-layouts  2.3 us (2%)
    pallas_call x1, Pallas kernels, per_device(): pl.pallas_call(kernel, out_shape=jax.ShapeDtypeStruct(queries.shape, BF16...  95 us
    unnamed x1, local copies, waits for them, and re-layouts  2.3 us

profile of v3, /device:TPU:192, one launch (start us, length us, event | category | flops | bytes accessed | tf_op | source)
XLA Modules:
  0.0 97.3 jit_solution(2235990843642508733)
XLA Ops:
  0.0 95.0 %shard_map.55 = bf16[256,2048]{1,0:T(8,128)(2,1)} custom-call(bf16[256,2048]{1,0:T(8,128)(2,1)} %q_ref.1, bf16[256,256]{1,0:T(8,128)(2,1)} %k_ref.1, bf16[256,256]{1,0:T(8,128)(2,1)} %v_ref.1, s32[1,2]{1,0:T(1,128)} %cnt_ref.1, s32[1,2,128]{2,1,0:T(2,128)} %rows_ref.1), custom_call_target="tpu_custom_call" | custom-call | flops 16999999488 | bytes 4000000 | tf_op jit(solution)/shard_map/pallas_call | solution.py:468
  95.0 2.3 %copy.7 = bf16[256,2048]{1,0:T(8,128)(2,1)} copy(bf16[256,2048]{1,0:T(8,128)(2,1)} %shard_map.55) | data formatting | bytes 2097152
